TPU v7x, 32 devices: a whole 2x2x4 slice. The times are simulated.
32 devices in a mesh: batch: 4 (over y, x), seq: 8 (over z, core).
Axes of the slice: x: 2, y: 2, z: 4, core: 2. Of those that a mesh axis runs over, the one named last changes fastest.
Arguments:
- block_in: bfloat16 [16, 1024, 1024], P('batch', 'seq'), may hold values from -6 to 6
- attn_in: bfloat16 [1024, 4096], P(None, 'seq'), may hold values from -0.1875 to 0.1875
- attn_out: bfloat16 [1024, 1024], P(None, 'seq'), may hold values from -0.375 to 0.375
- out_gain: bfloat16 [1024], P('seq'), may hold values from 0.5 to 1.5
- glu_in: bfloat16 [1024, 5632], P(None, 'seq'), may hold values from -0.1875 to 0.1875
- glu_out: bfloat16 [2816, 1024], P(None, 'seq'), may hold values from -0.109375 to 0.109375
- block_grad: bfloat16 [16, 1024, 1024], P('batch', 'seq'), may hold values from -6 to 6
Outputs:
- block_out: bfloat16 [16, 1024, 1024], P('batch', 'seq')
- input_grad: float32 [16, 1024, 1024], P('batch', 'seq')
- attn_in_grad: float32 [1024, 4096], P(None, 'seq')
- attn_out_grad: float32 [1024, 1024], P(None, 'seq')
- out_gain_grad: float32 [1024], P('seq')
- glu_in_grad: float32 [1024, 5632], P(None, 'seq')
- glu_out_grad: float32 [2816, 1024], P(None, 'seq')
All inputs are finite; a program needn't handle non-finite values.
Results may differ from a plain program's by a relative error of at most 0.02.
Values may be sent and summed in bfloat16 or wider, within the bound.
A program may use at most 320 MiB of HBM per device.

v0:
```python
import jax
import jax.numpy as jnp
from jax import lax
from jax.sharding import PartitionSpec as P

HEADS = 16
HEAD_DIM = 64
D = 1024
FF = 2816


def prefix(value, axis, combine, identity, reverse):
    devices, place = (lax.axis_size(axis), lax.axis_index(axis))
    everything = lax.all_gather(value.astype(jnp.bfloat16), axis)
    start = jnp.broadcast_to(jnp.asarray(identity, value.dtype), value.shape)

    def step(k, before):
        at = devices - 1 - k if reverse else k
        reached = at > place if reverse else at < place
        new = combine(before, everything[at].astype(value.dtype))
        return jnp.where(reached, new, before)

    return lax.fori_loop(0, devices, step, start)


def normalize(field, norm_eps):
    return field * lax.rsqrt(jnp.mean(field * field, axis=-1, keepdims=True) + norm_eps)


def normalize_back(field, grad_rows, norm_eps):
    row_scale = lax.rsqrt(jnp.mean(field * field, axis=-1, keepdims=True) + norm_eps)
    inner_mean = jnp.mean(grad_rows * field, axis=-1, keepdims=True)
    return row_scale * grad_rows - field * (row_scale * row_scale * row_scale) * inner_mean


def local(block_in, attn_in, attn_out, out_gain, glu_in, glu_out, block_grad):
    seq_count = block_in.shape[0]
    span_len = block_in.shape[1]
    row_count = seq_count * span_len
    w_attn_in, w_attn_out, gain_full, w_glu_in, w_glu_out = (
        lax.all_gather(attn_in, "seq", axis=1, tiled=True),
        lax.all_gather(attn_out, "seq", axis=1, tiled=True),
        lax.all_gather(out_gain, "seq", axis=0, tiled=True),
        lax.all_gather(glu_in, "seq", axis=1, tiled=True),
        lax.all_gather(glu_out, "seq", axis=1, tiled=True),
    )
    gain_wide = gain_full.astype(jnp.float32)
    source = block_in.reshape(row_count, D).astype(jnp.float32)
    norm_a = normalize(source, 1e-06).astype(jnp.bfloat16)
    projected = jnp.dot(norm_a, w_attn_in, preferred_element_type=jnp.float32)
    query_raw = projected[:, :D]
    key_raw = projected[:, D : 2 * D]
    value_raw = projected[:, 2 * D : 3 * D]
    gate_raw = projected[:, 3 * D :]
    queries = (
        jax.nn.softplus(query_raw)
        .astype(jnp.bfloat16)
        .reshape(seq_count, span_len, HEADS, HEAD_DIM)
    )
    keys_low = (
        jax.nn.softplus(key_raw).astype(jnp.bfloat16).reshape(seq_count, span_len, HEADS, HEAD_DIM)
    )
    values = value_raw.astype(jnp.bfloat16).reshape(seq_count, span_len, HEADS, HEAD_DIM)
    causal = jnp.tril(jnp.ones((span_len, span_len), dtype=bool))
    scores = jnp.einsum("bthe,bshe->bhts", queries, keys_low, preferred_element_type=jnp.float32)
    scores = jnp.where(causal, scores, 0.0).astype(jnp.bfloat16)
    local_state = jnp.einsum(
        "bthe,bthf->bhef", keys_low, values, preferred_element_type=jnp.float32
    )
    zero_state = jnp.zeros_like(local_state)
    earlier = prefix(local_state, "seq", jnp.add, zero_state, False)
    earlier_low = earlier.astype(jnp.bfloat16)
    attended = jnp.einsum("bhts,bshe->bthe", scores, values, preferred_element_type=jnp.float32)
    attended = attended + jnp.einsum(
        "bthe,bhef->bthf", queries, earlier_low, preferred_element_type=jnp.float32
    )
    head_scale = lax.rsqrt(jnp.mean(attended * attended, axis=-1, keepdims=True) + 1e-05)
    unit_rows = (attended * head_scale).reshape(row_count, D)
    normed = unit_rows * gain_wide
    gate_sig = jax.nn.sigmoid(gate_raw)
    gated_low = (gate_sig * normed).astype(jnp.bfloat16)
    middle = source + jnp.dot(gated_low, w_attn_out, preferred_element_type=jnp.float32)
    norm_b = normalize(middle, 1e-06).astype(jnp.bfloat16)
    glu_pair = jnp.dot(norm_b, w_glu_in, preferred_element_type=jnp.float32)
    gate_half = glu_pair[:, :FF]
    up_half = glu_pair[:, FF:]
    hidden = (gate_half * up_half).astype(jnp.bfloat16)
    result = middle + jnp.dot(hidden, w_glu_out, preferred_element_type=jnp.float32)
    block_out = result.astype(jnp.bfloat16).reshape(seq_count, span_len, D)
    grad_out = block_grad.reshape(row_count, D)
    glu_out_grad = jnp.einsum("rf,rd->fd", hidden, grad_out, preferred_element_type=jnp.float32)
    grad_hidden = jnp.einsum("rd,fd->rf", grad_out, w_glu_out, preferred_element_type=jnp.float32)
    grad_pair = jnp.concatenate([grad_hidden * up_half, grad_hidden * gate_half], axis=1).astype(
        jnp.bfloat16
    )
    glu_in_grad = jnp.einsum("rd,rf->df", norm_b, grad_pair, preferred_element_type=jnp.float32)
    grad_norm_b = jnp.einsum("rf,df->rd", grad_pair, w_glu_in, preferred_element_type=jnp.float32)
    grad_middle = grad_out.astype(jnp.float32) + normalize_back(middle, grad_norm_b, 1e-06)
    grad_branch = grad_middle.astype(jnp.bfloat16)
    attn_out_grad = jnp.einsum(
        "rk,rd->kd", gated_low, grad_branch, preferred_element_type=jnp.float32
    )
    grad_gated = jnp.einsum(
        "rd,kd->rk", grad_branch, w_attn_out, preferred_element_type=jnp.float32
    )
    grad_normed = grad_gated * gate_sig
    grad_gate = grad_gated * normed * gate_sig * (1.0 - gate_sig)
    gain_grad = jnp.sum(grad_normed * unit_rows, axis=0)
    grad_unit = (grad_normed * gain_wide).reshape(seq_count, span_len, HEADS, HEAD_DIM)
    head_inner = jnp.mean(grad_unit * attended, axis=-1, keepdims=True)
    grad_attended = (
        head_scale * grad_unit - attended * (head_scale * head_scale * head_scale) * head_inner
    ).astype(jnp.bfloat16)
    grad_scores = jnp.einsum(
        "bthf,bshf->bhts", grad_attended, values, preferred_element_type=jnp.float32
    )
    grad_scores = jnp.where(causal, grad_scores, 0.0).astype(jnp.bfloat16)
    state_grad = jnp.einsum(
        "bthe,bthf->bhef", queries, grad_attended, preferred_element_type=jnp.float32
    )
    later_sum = prefix(state_grad, "seq", jnp.add, zero_state, True)
    later_low = later_sum.astype(jnp.bfloat16)
    grad_query = jnp.einsum(
        "bhts,bshe->bthe", grad_scores, keys_low, preferred_element_type=jnp.float32
    )
    grad_query = grad_query + jnp.einsum(
        "bthf,bhef->bthe", grad_attended, earlier_low, preferred_element_type=jnp.float32
    )
    grad_key = jnp.einsum(
        "bhts,bthe->bshe", grad_scores, queries, preferred_element_type=jnp.float32
    )
    grad_key = grad_key + jnp.einsum(
        "bthf,bhef->bthe", values, later_low, preferred_element_type=jnp.float32
    )
    grad_value = jnp.einsum(
        "bhts,bthf->bshf", scores, grad_attended, preferred_element_type=jnp.float32
    )
    grad_value = grad_value + jnp.einsum(
        "bthe,bhef->bthf", keys_low, later_low, preferred_element_type=jnp.float32
    )
    grad_proj = jnp.concatenate(
        [
            grad_query.reshape(row_count, D) * jax.nn.sigmoid(query_raw),
            grad_key.reshape(row_count, D) * jax.nn.sigmoid(key_raw),
            grad_value.reshape(row_count, D),
            grad_gate,
        ],
        axis=1,
    ).astype(jnp.bfloat16)
    attn_in_grad = jnp.einsum("rd,rk->dk", norm_a, grad_proj, preferred_element_type=jnp.float32)
    grad_norm_a = jnp.einsum("rk,dk->rd", grad_proj, w_attn_in, preferred_element_type=jnp.float32)
    input_grad = grad_middle + normalize_back(source, grad_norm_a, 1e-06)
    grad_parts = (
        lax.psum_scatter(
            attn_in_grad.astype(jnp.bfloat16), "seq", scatter_dimension=1, tiled=True
        ).astype(jnp.float32),
        lax.psum_scatter(
            attn_out_grad.astype(jnp.bfloat16), "seq", scatter_dimension=1, tiled=True
        ).astype(jnp.float32),
        lax.psum_scatter(
            gain_grad.astype(jnp.bfloat16), "seq", scatter_dimension=0, tiled=True
        ).astype(jnp.float32),
        lax.psum_scatter(
            glu_in_grad.astype(jnp.bfloat16), "seq", scatter_dimension=1, tiled=True
        ).astype(jnp.float32),
        lax.psum_scatter(
            glu_out_grad.astype(jnp.bfloat16), "seq", scatter_dimension=1, tiled=True
        ).astype(jnp.float32),
    )
    totals = (
        lax.psum(grad_parts[0].astype(jnp.bfloat16), "batch").astype(jnp.float32),
        lax.psum(grad_parts[1].astype(jnp.bfloat16), "batch").astype(jnp.float32),
        lax.psum(grad_parts[2].astype(jnp.bfloat16), "batch").astype(jnp.float32),
        lax.psum(grad_parts[3].astype(jnp.bfloat16), "batch").astype(jnp.float32),
        lax.psum(grad_parts[4].astype(jnp.bfloat16), "batch").astype(jnp.float32),
    )
    final_grads = (totals[0], totals[1], totals[2], totals[3], totals[4])
    return (
        block_out,
        input_grad.reshape(seq_count, span_len, D),
        final_grads[0],
        final_grads[1],
        final_grads[2],
        final_grads[3],
        final_grads[4],
    )


def solution(mesh):
    placed = (
        P("batch", "seq", None),
        P(None, "seq"),
        P(None, "seq"),
        P("seq"),
        P(None, "seq"),
        P(None, "seq"),
        P("batch", "seq", None),
    )
    return jax.shard_map(
        local,
        mesh=mesh,
        in_specs=placed,
        out_specs=(
            P("batch", "seq", None),
            P("batch", "seq", None),
            P(None, "seq"),
            P(None, "seq"),
            P("seq"),
            P(None, "seq"),
            P(None, "seq"),
        ),
        check_vma=False,
    )
```

profile of v0, /device:TPU:0, one launch (start us, length us, event | category | flops | bytes accessed | tf_op | source)
XLA Modules:
  0.0 951.5 jit_solution(16775001569131298390)
XLA Ops:
  10.9 83.5 %all-gather.10.cloned.1.call-done = bf16[1024,4096]{1,0:T(8,128)(2,1)} async-done(((bf16[1024,512]{1,0:T(8,128)(2,1)}), bf16[1024,4096]{1,0:T(8,128)(2,1)}) %all-gather.10.cloned.1.call-update) | async-done | bytes 8388624 | tf_op jit(solution)/shard_map/all_gather | solution.py:41
  94.4 6.9 fusion.31
  121.8 9.1 all-gather.2
  145.1 55.4 %all-gather.18.cloned.1.call-done = bf16[32,16,64,64]{3,2,1,0:T(8,128)(2,1)} async-done(((bf16[4,16,64,64]{3,2,1,0:T(8,128)(2,1)}), bf16[32,16,64,64]{3,2,1,0:T(8,128)(2,1)}) %all-gather.18.cloned.1.call-update) | async-done | bytes 4194320 | tf_op jit(solution)/shard_map/all_gather | solution.py:14
  200.5 20.4 %while.30 = (s32[]{:T(128)}, f32[4,16,64,64]{3,2,1,0:T(8,128)S(1)}, s32[]{:T(128)}, bf16[8,4,16,64,64]{4,3,2,1,0:T(8,128)(2,1)}, s32[]{:T(128)}, /*index=5*/s32[]{:T(128)}) while((s32[]{:T(128)}, f32[4,16,64,64]{3,2,1,0:T(8,128)S(1)}, s32[]{:T(128)}, bf16[8,4,16,64,64]{4,3,2,1,0:T(8,128)(2,1)}, s32[]{:T(128)}, ...), condition=%wide.region_2.3_spmd.clone, body=%wide.region_1.2_spmd.clone.sunk | while | flops 1048580 | bytes 2621541 | solution.py:23
  230.4 4.8 reshape.153
  239.1 5.3 multiply_reduce_fusion.2
  244.3 95.8 %all-gather.14.cloned.1.call-done = bf16[1024,5632]{0,1:T(8,128)(2,1)} async-done(((bf16[1024,704]{0,1:T(8,128)(2,1)}), bf16[1024,5632]{0,1:T(8,128)(2,1)}) %all-gather.14.cloned.1.call-update) | async-done | bytes 11534352 | tf_op jit(solution)/shard_map/all_gather | solution.py:44
  340.2 12.6 %fusion.30 = f32[512,5632]{1,0:T(8,128)} fusion(bf16[1024,5632]{0,1:T(8,128)(2,1)} %all-gather.14.cloned.1.call-done, f32[512,1024]{1,0:T(8,128)} %get-tuple-element.265, f32[512]{0:T(512)S(1)} %get-tuple-element.261), kind=kOutput, calls=%fused_computation.83 | convolution fusion | flops 5906628608 | bytes 25167872 | tf_op jit(solution)/shard_map/dot_general | solution.py:84
  352.8 48.0 %all-gather.16.cloned.1.call-done = bf16[2816,1024]{1,0:T(8,128)(2,1)} async-done(((bf16[2816,128]{1,0:T(8,128)(2,1)}), bf16[2816,1024]{1,0:T(8,128)(2,1)}) %all-gather.16.cloned.1.call-update) | async-done | bytes 5767184 | tf_op jit(solution)/shard_map/all_gather | solution.py:45
  400.8 13.3 %multiply_convert_fusion.1 = (bf16[512,2816]{1,0:T(8,128)(2,1)}, bf16[512,2816]{1,0:T(8,128)(2,1)}, bf16[512,2816]{1,0:T(8,128)(2,1)}) fusion(f32[512,5632]{1,0:T(8,128)} %fusion.30, bf16[512,1024]{1,0:T(8,128)(2,1)} %bitcast.112, bf16[2816,1024]{1,0:T(8,128)(2,1)} %all-gather.16.cloned.1.call-done), kind=kOutput, calls=%fused_computation.8 | convolution fusion | flops 2961440768 | bytes 27000832 | tf_op jit(solution)/shard_map/rd,fd->rf/dot_general | solution.py:92
  414.1 10.9 %multiply_reduce_fusion.1 = (f32[512]{0:T(512)S(1)}, f32[512,1024]{1,0:T(8,128)S(1)}) fusion(f32[512,1024]{1,0:T(8,128)S(1)} %copy-done.21, bf16[1024,5632]{0,1:T(8,128)(2,1)} %all-gather.14.cloned.1.call-done, bf16[512,2816]{1,0:T(8,128)(2,1)} %get-tuple-element.249, bf16[512,2816]{1,0:T(8,128)(2,1)} %get-tuple-element.248), kind=kOutput, calls=%fused_computation.50 | convolution fusion | flops 5918162432 | bytes 21497856 | tf_op jit(solution)/shard_map/rf,df->rd/dot_general | solution.py:97
  427.2 5.9 multiply_reduce_fusion
  433.1 4.5 reshape.154
  448.6 4.6 convolution_convert_fusion.3
  457.6 7.8 convolution_convert_fusion.2
  465.4 8.5 copy.99
  473.9 12.2 %convolution_convert_fusion = bf16[1024,5632]{0,1:T(8,128)(2,1)} fusion(bf16[512,2816]{1,0:T(8,128)(2,1)} %get-tuple-element.249, bf16[512,2816]{1,0:T(8,128)(2,1)} %get-tuple-element.248, f32[512,1024]{1,0:T(8,128)} %get-tuple-element.265, f32[512]{0:T(512)S(1)} %get-tuple-element.261), kind=kOutput, calls=%fused_computation.2 | convolution fusion | flops 5923930112 | bytes 19400704 | tf_op jit(solution)/shard_map/rd,rf->df/dot_general | solution.py:96
  496.3 5.0 reshape.142
  507.1 21.9 %all-gather.20.cloned.1.call-done = bf16[32,16,64,64]{3,2,1,0:T(8,128)(2,1)} async-done(((bf16[4,16,64,64]{3,2,1,0:T(8,128)(2,1)}), bf16[32,16,64,64]{3,2,1,0:T(8,128)(2,1)}) %all-gather.20.cloned.1.call-update) | async-done | bytes 4194320 | tf_op jit(solution)/shard_map/all_gather | solution.py:14
  529.0 20.4 %while.31 = (s32[]{:T(128)}, f32[4,16,64,64]{3,2,1,0:T(8,128)S(1)}, s32[]{:T(128)}, bf16[8,4,16,64,64]{4,3,2,1,0:T(8,128)(2,1)}, s32[]{:T(128)}, /*index=5*/s32[]{:T(128)}, s32[]{:T(128)}, s32[]{:T(128)}) while((s32[]{:T(128)}, f32[4,16,64,64]{3,2,1,0:T(8,128)S(1)}, s32[]{:T(128)}, bf16[8,4,16,64,64]{4,3,2,1,0:T(8,128)(2,1)}, ...), condition=%wide.region_8.9_spmd.clone, body=%wide.region_7.8_spmd.clone.sunk | while | flops 1048584 | bytes 2621603 | solution.py:23
  567.8 5.0 reshape.143
  572.8 4.2 multiply_convert_fusion.5
  578.3 7.7 convolution_convert_fusion.1
  587.8 43.8 %reduce-scatter.15.cloned.1.call-done = bf16[128,2816]{1,0:T(8,128)(2,1)} async-done(((bf16[1024,2816]{1,0:T(8,128)(2,1)}), bf16[128,2816]{1,0:T(8,128)(2,1)}) %reduce-scatter.15.cloned.1.call-update) | async-done | bytes 720912
  633.9 117.7 %reduce-scatter.11.cloned.1.call-done = bf16[1024,704]{0,1:T(8,128)(2,1)} async-done(((bf16[1024,5632]{0,1:T(8,128)(2,1)}), bf16[1024,704]{0,1:T(8,128)(2,1)}) %reduce-scatter.11.cloned.1.call-update) | async-done | bytes 1441808 | tf_op jit(solution)/shard_map/reduce_scatter | solution.py:163
  751.6 90.2 %reduce-scatter.9.cloned.1.call-done = bf16[1024,512]{1,0:T(8,128)(2,1)} async-done(((bf16[1024,4096]{1,0:T(8,128)(2,1)}), bf16[1024,512]{1,0:T(8,128)(2,1)}) %reduce-scatter.9.cloned.1.call-update) | async-done | bytes 1048592 | tf_op jit(solution)/shard_map/reduce_scatter | solution.py:154
  843.1 13.6 %all-reduce = bf16[1024]{0:T(1024)(128)(2,1)S(1)} all-reduce(bf16[1024]{0:T(1024)(128)(2,1)S(1)} %get-tuple-element.250), channel_id=6, replica_groups=mesh['batch'=4,'seq'=8] {'seq'}, use_global_device_ids=true, to_apply=%region_15.16.clone | all-reduce | flops 1024 | bytes 4096
  856.8 10.2 %psum.37 = bf16[128]{0:T(256)(128)(2,1)S(1)} all-reduce(bf16[128]{0:T(256)(128)(2,1)S(1)} %dynamic-slice.1), channel_id=1, replica_groups=mesh['batch'=4,'seq'=8] {'batch'}, use_global_device_ids=true, to_apply=%region_16.17 | all-reduce | flops 128 | bytes 512 | tf_op jit(solution)/shard_map/psum | solution.py:173
  867.5 7.8 add_convert_fusion.1
  875.4 8.8 fusion.16
  886.0 51.6 %all-reduce.4.cloned.1.call-done = (bf16[1024,512]{1,0:T(8,128)(2,1)}, bf16[1024,128]{1,0:T(8,128)(2,1)}, bf16[1024,704]{0,1:T(8,128)(2,1)}, bf16[2816,128]{1,0:T(8,128)(2,1)}) async-done(((bf16[1024,512]{1,0:T(8,128)(2,1)}, bf16[1024,128]{1,0:T(8,128)(2,1)}, bf16[1024,704]{0,1:T(8,128)(2,1)}, bf16[2816,128]{1,0:T(8,128)(2,1)}), (bf16[1024,512]{1,0:T(8,128)(2,1)}, bf16[1024,128]{1,0:T(8,128)(2,1)}, ...) | async-done | bytes 3473424 | tf_op jit(solution)/shard_map/psum | solution.py:171
  (183 shorter events, 159.3 us)
Async XLA Ops:
  7.2 87.2 %all-gather.10.cloned.1.call-start = ((), (), s32[]{:S(2)}) async-start(), calls=%async_computation.4 | async-start | bytes 9437184 | tf_op jit(solution)/shard_map/all_gather | solution.py:41
  7.9 192.6 %all-gather.18.cloned.1.call-start = ((), (), s32[]{:S(2)}) async-start(), calls=%async_computation.10 | async-start | bytes 9437184 | tf_op jit(solution)/shard_map/all_gather | solution.py:14
  10.9 90.4 %copy-start.30 = (bf16[512,1024]{1,0:T(8,128)(2,1)}, bf16[512,1024]{1,0:T(8,128)(2,1)S(1)}, u32[]{:S(2)}) copy-start(bf16[512,1024]{1,0:T(8,128)(2,1)S(1)} %fusion.12) | copy-start | bytes 3145732
  119.8 119.3 %all-gather.12.cloned.1.call-start = ((), (), s32[]{:S(2)}) async-start(), calls=%async_computation.5 | async-start | bytes 2359296 | tf_op jit(solution)/shard_map/all_gather | solution.py:42
  120.5 219.7 %all-gather.14.cloned.1.call-start = ((), (), s32[]{:S(2)}) async-start(), calls=%async_computation.6 | async-start | bytes 12976128 | tf_op jit(solution)/shard_map/all_gather | solution.py:44
  121.1 279.7 %all-gather.16.cloned.1.call-start = ((), (), s32[]{:S(2)}) async-start(), calls=%async_computation.7 | async-start | bytes 6488064 | tf_op jit(solution)/shard_map/all_gather | solution.py:45
  121.7 407.3 %all-gather.20.cloned.1.call-start = ((), (), s32[]{:S(2)}) async-start(), calls=%async_computation.11 | async-start | bytes 9437184 | tf_op jit(solution)/shard_map/all_gather | solution.py:14
  400.8 13.3 %copy-start.21 = (f32[512,1024]{1,0:T(8,128)S(1)}, f32[512,1024]{1,0:T(8,128)}, u32[]{:S(2)}) copy-start(f32[512,1024]{1,0:T(8,128)} %get-tuple-element.265) | copy-start | bytes 6291460
  414.1 10.9 %copy-start.32 = (bf16[4,128,1024]{2,1,0:T(8,128)(2,1)S(1)}, bf16[4,128,1024]{2,1,0:T(8,128)(2,1)}, u32[]{:S(2)}) copy-start(bf16[4,128,1024]{2,1,0:T(8,128)(2,1)} %param.17) | copy-start | bytes 3145732
  427.2 5.9 copy-start.19
  448.6 137.4 %reduce-scatter.13.cloned.1.call-start = ((), (), s32[]{:S(2)}) async-start(), calls=%async_computation.12 | async-start | bytes 2359296
  457.4 174.2 %reduce-scatter.15.cloned.1.call-start = ((), (), s32[]{:S(2)}) async-start(), calls=%async_computation.13 | async-start | bytes 6488064
  473.9 277.8 %reduce-scatter.11.cloned.1.call-start = ((), (), s32[]{:S(2)}) async-start(), calls=%async_computation.9 | async-start | bytes 12976128 | tf_op jit(solution)/shard_map/reduce_scatter | solution.py:163
  486.1 355.6 %reduce-scatter.9.cloned.1.call-start = ((), (), s32[]{:S(2)}) async-start(), calls=%async_computation.8 | async-start | bytes 9437184 | tf_op jit(solution)/shard_map/reduce_scatter | solution.py:154
  496.3 5.0 copy-start.9
  505.1 23.9 %copy-start = (f32[4,16,64,64]{3,2,1,0:T(8,128)S(1)}, f32[4,16,64,64]{3,2,1,0:T(8,128)}, u32[]{:S(2)}) copy-start(f32[4,16,64,64]{3,2,1,0:T(8,128)} %custom-call.1) | copy-start | bytes 3145732
  567.8 5.0 copy-start.17
  572.8 5.5 copy-start.24
  572.8 5.5 copy-start.31
  572.8 5.5 copy-start.42
  586.0 351.6 %all-reduce.4.cloned.1.call-start = ((), (), s32[]{:S(2)}) async-start(), calls=%async_computation.14 | async-start | bytes 6946816 | tf_op jit(solution)/shard_map/psum | solution.py:171
  633.9 207.9 %copy-start.41 = (u32[32]{0:T(128)S(1)}, u32[32]{0:T(128)}, u32[]{:S(2)}) copy-start(u32[32]{0:T(128)} %constant.97) | copy-start | bytes 388
  633.9 209.2 %copy-start.36 = (f32[4,128]{1,0:T(4,128)S(1)}, f32[4,128]{1,0:T(4,128)}, u32[]{:S(2)}) copy-start(f32[4,128]{1,0:T(4,128)} %copy-done.35) | copy-start | bytes 6148
  633.9 233.6 %copy-start.22 = (f32[512,1024]{1,0:T(8,128)S(1)}, f32[512,1024]{1,0:T(8,128)}, u32[]{:S(2)}) copy-start(f32[512,1024]{1,0:T(8,128)} %get-tuple-element.265) | copy-start | bytes 6291460
  867.5 7.8 copy-start.16
  867.5 7.8 copy-start.25
  867.5 7.8 copy-start.27
  867.5 7.8 copy-start.29
  867.5 7.8 copy-start.43
  875.4 8.8 copy-start.20
  875.4 8.8 copy-start.38
  937.6 3.8 copy-start.23
  (23 other events, 47.7 us)
Sparse Core Ops, SparseCore 0:
  9.6 84.7 all-gather.9
  119.9 80.5 all-gather.17
  202.1 29.3 all-gather.11
  233.0 107.1 all-gather.13
  341.6 59.1 all-gather.15
  448.7 80.2 all-gather.19
  531.3 34.3 reduce-scatter.12
  568.0 63.5 reduce-scatter.14
  633.9 117.6 reduce-scatter.10
  753.8 87.9 reduce-scatter.8
  845.8 91.7 all-reduce.3
where the time goes:
time: 960 us; the launch traced here: 951 us
  waiting for transfers between devices  610 us (64%)
  matrix products  133 us (14%)
  local copies, waits for them, and re-layouts  89.8 us (9%)
  other arithmetic  68.9 us (7%)
  blocking collectives  33 us (3%)
  between operations  15.5 us (2%)
    reduce_scatter x1, waiting for transfers between devices, local(): lax.psum_scatter(glu_in_grad.astype(jnp.bfloat16), 'seq', scatter_dimensi...  118 us
    all_gather x1, waiting for transfers between devices, local(): lax.all_gather(glu_in, 'seq', axis=1, tiled=True)  95.8 us
    reduce_scatter x1, waiting for transfers between devices, local(): lax.psum_scatter(attn_in_grad.astype(jnp.bfloat16), 'seq', scatter_dimens...  90.2 us
    all_gather x1, waiting for transfers between devices, local(): lax.all_gather(attn_in, 'seq', axis=1, tiled=True)  83.5 us
    all_gather x2, waiting for transfers between devices, prefix(): everything = lax.all_gather(value.astype(jnp.bfloat16), axis)  77.3 us
    psum x1, waiting for transfers between devices, local(): lax.psum(grad_parts[0].astype(jnp.bfloat16), 'batch').astype(jnp.float32)  51.6 us
    all_gather x1, waiting for transfers between devices, local(): lax.all_gather(glu_out, 'seq', axis=1, tiled=True)  48 us
    unnamed x13, waiting for transfers between devices  46.3 us
  transfers between devices with their start and end apart: 11, of which 9 were waited for; matrix products, arithmetic and copies ran while one was open for 22% of the time, Pallas kernels for 0%

commit v1 on v0

v1 whole, which is shorter than its diff:
```python
import functools

import jax
import jax.numpy as jnp
from jax import lax
from jax.experimental import pallas as pl
from jax.experimental.pallas import tpu as pltpu
from jax.sharding import PartitionSpec as P

HEADS = 16
HEAD_DIM = 64
D = 1024
FF = 2816
MESH = pl.DeviceIdType.MESH
BF16 = jnp.bfloat16
F32 = jnp.float32
PAD_ROWS = 16
GAIN_ROWS = 128


def run_if(cond, fn):
    if cond is None:
        fn()
    else:
        pl.when(cond)(fn)


class Place:
    def __init__(self, batch, seq):
        self.planes = seq // 2
        self.square = batch == 4
        self.b = lax.axis_index("batch")
        self.s = lax.axis_index("seq")
        self.z = lax.div(self.s, 2)
        self.c = lax.rem(self.s, 2)
        self.bx = self.b + 1 - 2 * lax.rem(self.b, 2)
        self.by = lax.rem(self.b + 2, 4)
        self.bd = lax.rem(self.bx + 2, 4)
        self.sib = (self.b, self.s + 1 - 2 * self.c)
        self.up = (self.b, self.s + 2)
        self.down = (self.b, self.s - 2)
        self.x = (self.bx, self.s)
        self.y = (self.by, self.s)
        self.has_up = self.z < self.planes - 1
        self.has_down = self.z > 0
        self.sent = []

    def barrier(self):
        sem = pltpu.get_barrier_semaphore()
        always = [self.sib] + ([self.x, self.y] if self.square else [])
        for device in always:
            pl.semaphore_signal(sem, inc=1, device_id=device, device_id_type=MESH)
        for cond, device in ((self.has_up, self.up), (self.has_down, self.down)):
            pl.when(cond)(
                lambda device=device: pl.semaphore_signal(
                    sem, inc=1, device_id=device, device_id_type=MESH
                )
            )
        ends = self.has_up.astype(jnp.int32) + self.has_down.astype(jnp.int32)
        pl.semaphore_wait(sem, len(always) + ends)

    def copy(self, src, dst, send_sem, recv_sem, device):
        return pltpu.make_async_remote_copy(
            src_ref=src,
            dst_ref=dst,
            send_sem=send_sem,
            recv_sem=recv_sem,
            device_id=device,
            device_id_type=MESH,
        )

    def send(self, make, cond=None):
        run_if(cond, lambda: make().start())
        self.sent.append((cond, make))

    def finish(self):
        for cond, make in self.sent:
            run_if(cond, lambda make=make: make().wait_send())
        self.sent = []


class Gather:
    Z_UP, Z_DOWN, Z_IN, X_OUT, X_IN, Y_OUT, Y_IN, FX_OUT, FX_IN, FY_OUT, FY_IN, S_OUT, S_IN = range(13)
    KINDS = 13

    def __init__(self, place, shards, fulls, quartered, sems, local_sems):
        self.p, self.shards, self.fulls, self.sems = place, shards, fulls, sems
        self.local_sems = local_sems
        self.quartered = [q and place.square for q in quartered]

    def rows(self, w, owner, half=None):
        rows = self.shards[w].shape[0]
        if not self.quartered[w]:
            return pl.ds(0, rows)
        part = rows // 4
        if half is None:
            return pl.ds(pl.multiple_of(owner * part, 16), part)
        return pl.ds(pl.multiple_of(owner * part + half * (part // 2), 16), part // 2)

    def move(self, w, zz, rows, out, into, device):
        block = self.fulls[w].at[2 * zz + self.p.c, rows]
        return self.p.copy(
            block, block, self.sems.at[out, w, zz], self.sems.at[into, w, zz], device
        )

    def start(self, w):
        p, own = self.p, self.shards[w]
        here = self.fulls[w].at[p.s]
        rows = self.rows(w, p.b)
        for cond, device, out in (
            (p.has_up, p.up, self.Z_UP),
            (p.has_down, p.down, self.Z_DOWN),
        ):
            p.send(
                lambda device=device, out=out: p.copy(
                    own.at[rows],
                    here.at[rows],
                    self.sems.at[out, w, p.z],
                    self.sems.at[self.Z_IN, w, p.z],
                    device,
                ),
                cond,
            )
        p.send(
            lambda: p.copy(
                own, here, self.sems.at[self.S_OUT, w, p.z], self.sems.at[self.S_IN, w, p.z], p.sib
            )
        )
        pltpu.make_async_copy(own, here, self.local_sems.at[w]).start()

    def sides(self, d):
        p = self.p
        return (
            (p.z >= d, p.z - d, p.has_up, p.up, self.Z_UP),
            (p.z + d < p.planes, p.z + d, p.has_down, p.down, self.Z_DOWN),
        )

    def from_z(self, w, d):
        p = self.p
        rows = self.rows(w, p.b)
        for cond, zz, more, device, out in self.sides(d):
            run_if(
                cond, lambda zz=zz: self.move(w, zz, rows, self.Z_UP, self.Z_IN, p.up).wait_recv()
            )
            p.send(
                lambda zz=zz, device=device, out=out: self.move(
                    w, zz, rows, out, self.Z_IN, device
                ),
                jnp.logical_and(cond, more),
            )
            if self.quartered[w]:
                p.send(lambda zz=zz: self.move(w, zz, rows, self.X_OUT, self.X_IN, p.x), cond)
                p.send(lambda zz=zz: self.move(w, zz, rows, self.Y_OUT, self.Y_IN, p.y), cond)

    def from_plane(self, w, d):
        p = self.p
        if not self.quartered[w]:
            return
        from_x, from_y = self.rows(w, p.bx), self.rows(w, p.by)
        half_x, half_y = self.rows(w, p.bx, 0), self.rows(w, p.by, 1)
        for cond, zz, *_ in self.sides(d):
            run_if(
                cond, lambda zz=zz: self.move(w, zz, from_x, self.X_OUT, self.X_IN, p.x).wait_recv()
            )
            p.send(lambda zz=zz: self.move(w, zz, half_x, self.FY_OUT, self.FY_IN, p.y), cond)
            run_if(
                cond, lambda zz=zz: self.move(w, zz, from_y, self.Y_OUT, self.Y_IN, p.y).wait_recv()
            )
            p.send(lambda zz=zz: self.move(w, zz, half_y, self.FX_OUT, self.FX_IN, p.x), cond)

    def from_diagonal(self, w, d):
        p = self.p
        half_0, half_1 = self.rows(w, p.bd, 0), self.rows(w, p.bd, 1)
        for cond, zz, *_ in self.sides(d):
            if self.quartered[w]:
                run_if(
                    cond,
                    lambda zz=zz: self.move(w, zz, half_0, self.FY_OUT, self.FY_IN, p.y).wait_recv(),
                )
                run_if(
                    cond,
                    lambda zz=zz: self.move(w, zz, half_1, self.FX_OUT, self.FX_IN, p.x).wait_recv(),
                )
            p.send(lambda zz=zz: self.whole(w, zz, p.c), cond)

    def whole(self, w, zz, core):
        block = self.fulls[w].at[2 * zz + core]
        return self.p.copy(
            block, block, self.sems.at[self.S_OUT, w, zz], self.sems.at[self.S_IN, w, zz], self.p.sib
        )

    def from_sibling(self, w):
        p = self.p
        pltpu.make_async_copy(
            self.shards[w], self.fulls[w].at[p.s], self.local_sems.at[w]
        ).wait()
        for zz in range(p.planes):
            self.whole(w, zz, 1 - p.c).wait_recv()


def plan_gather(g, count):
    far = g.p.planes - 1
    steps = [lambda: g.start(0)]

    def add(fn, *args):
        step = functools.partial(fn, *args)
        step.whole = fn.__name__ == "from_sibling"
        steps.append(step)

    for w in range(count):
        for d in range(1, far + 1):
            if not (d == 1 and w > 0):
                add(g.from_z, w, d)
            if d == max(far - 1, 1) and w + 1 < count:
                add(g.start, w + 1)
            if d >= 2:
                add(g.from_plane, w, d - 1)
            if d >= 3:
                add(g.from_diagonal, w, d - 2)
        if w + 1 < count:
            add(g.from_z, w + 1, 1)
        add(g.from_plane, w, far)
        if far >= 2:
            add(g.from_diagonal, w, far - 1)
        add(g.from_diagonal, w, far)
        add(g.from_sibling, w)
    return steps


def add_into(dst, src, row, rows):
    cols = dst.shape[-1]
    chunk = max(
        k for k in range(16, rows + 1, 16) if rows % k == 0 and (k * cols <= 49152 or k == 16)
    )

    def body(i, _):
        here = pl.ds(pl.multiple_of(row + i * chunk, 16), chunk)
        there = pl.ds(pl.multiple_of(i * chunk, 16), chunk)
        dst[here, :] = (dst[here, :].astype(F32) + src[there, :].astype(F32)).astype(BF16)
        return 0

    lax.fori_loop(0, rows // chunk, body, 0)


class Reduce:
    (X1_OUT, X1_IN, Y1_OUT, Y1_IN, X2_OUT, X2_IN, Y2_OUT, Y2_IN, X3_OUT, X3_IN, Y3_OUT, Y3_IN) = range(12)
    KINDS = 12
    S_OUT, S_IN = range(2)
    Z_UP, Z_UP_IN, Z_DOWN, Z_DOWN_IN, FETCH = range(5)
    GX_OUT, GX_IN, GY_OUT, GY_IN, FX_OUT, FX_IN, FY_OUT, FY_IN, LOCAL = range(9)
    LAST_KINDS = 9

    def __init__(self, place, wide, z_parts, out, zin_far, refs):
        self.p, self.wide, self.out = place, wide and place.square, out
        self.part, self.x1, self.y1, self.x2, self.y2, zin, self.stage = refs[:7]
        self.core_sems, self.sems, self.z_sems, self.last_sems = refs[7:]
        self.zin = zin if self.wide else zin_far
        self.total = self.part.shape[1]
        self.quarter, self.half = self.total // 4, self.total // 8
        self.z_parts = 1 if self.wide else z_parts

    @staticmethod
    def scratch(square, wide, planes, rows, cols, core_parts, z_parts):
        wide = wide and square
        pieces = planes if wide else 1
        small = (pieces, rows // 8, cols) if square else (1, 16, 128)
        large = (pieces, rows // 4, cols) if square else (1, 16, 128)
        return [
            pltpu.VMEM((planes, rows, cols), BF16),
            pltpu.VMEM(small, BF16),
            pltpu.VMEM(small, BF16),
            pltpu.VMEM(large, BF16),
            pltpu.VMEM(large, BF16),
            pltpu.VMEM((planes + 1, rows // 4, cols) if wide else (1, 16, 128), BF16),
            pltpu.VMEM((16, 128) if wide else (rows // z_parts, cols), BF16),
            pltpu.SemaphoreType.DMA((2, planes, core_parts)),
            pltpu.SemaphoreType.DMA((Reduce.KINDS, pieces)),
            pltpu.SemaphoreType.DMA((5, planes + 1, z_parts)),
            pltpu.SemaphoreType.DMA((Reduce.LAST_KINDS,)),
        ]

    @staticmethod
    def far(square, wide, planes, rows, cols):
        shape = (1, 16, 128) if wide and square else (planes + 1, rows, cols)
        return jax.ShapeDtypeStruct(shape, BF16)

    def at(self, owner, half=None):
        if half is None:
            return pl.ds(pl.multiple_of(owner * self.quarter, 16), self.quarter)
        return pl.ds(pl.multiple_of(owner * self.quarter + half * self.half, 16), self.half)

    def sem(self, kind, k):
        return self.sems.at[kind, k]

    def core_copy(self, zz, src, row, rows, k):
        block = self.part.at[zz, pl.ds(row, rows)]
        return self.p.copy(
            block if src is None else src,
            block,
            self.core_sems.at[self.S_OUT, zz, k],
            self.core_sems.at[self.S_IN, zz, k],
            self.p.sib,
        )

    def slot(self, zz):
        return zz if self.wide else 0

    def hop(self, zz, rows, dst, out, into, device):
        return self.p.copy(
            self.part.at[zz, rows],
            dst,
            self.sem(out, self.slot(zz)),
            self.sem(into, self.slot(zz)),
            device,
        )

    def plane_1(self, zz):
        p, k, h = self.p, self.slot(zz), self.half
        lo, hi = pl.ds(0, h), pl.ds(h, h)
        p.send(lambda: self.hop(zz, self.at(p.bd, 0), self.x1.at[k], self.X1_OUT, self.X1_IN, p.x))
        p.send(lambda: self.hop(zz, self.at(p.bd, 1), self.y1.at[k], self.Y1_OUT, self.Y1_IN, p.y))
        p.send(lambda: self.hop(zz, self.at(p.bx, 0), self.x2.at[k, lo], self.X2_OUT, self.X2_IN, p.x))
        p.send(lambda: self.hop(zz, self.at(p.by, 1), self.y2.at[k, hi], self.Y2_OUT, self.Y2_IN, p.y))

    def plane_2(self, zz):
        p, k, h = self.p, self.slot(zz), self.half
        lo, hi = pl.ds(0, h), pl.ds(h, h)
        self.hop(zz, self.at(p.bd, 0), self.x1.at[k], self.X1_OUT, self.X1_IN, p.x).wait_recv()
        add_into(self.part.at[zz], self.x1.at[k], p.by * self.quarter, h)
        p.send(lambda: self.hop(zz, self.at(p.by, 0), self.y2.at[k, lo], self.Y3_OUT, self.Y3_IN, p.y))
        self.hop(zz, self.at(p.bd, 1), self.y1.at[k], self.Y1_OUT, self.Y1_IN, p.y).wait_recv()
        add_into(self.part.at[zz], self.y1.at[k], p.bx * self.quarter + h, h)
        p.send(lambda: self.hop(zz, self.at(p.bx, 1), self.x2.at[k, hi], self.X3_OUT, self.X3_IN, p.x))

    def plane_3(self, zz):
        p, k, h = self.p, self.slot(zz), self.half
        lo, hi = pl.ds(0, h), pl.ds(h, h)
        self.hop(zz, self.at(p.bx, 0), self.x2.at[k, lo], self.X2_OUT, self.X2_IN, p.x).wait_recv()
        self.hop(zz, self.at(p.by, 1), self.y2.at[k, hi], self.Y2_OUT, self.Y2_IN, p.y).wait_recv()
        self.hop(zz, self.at(p.bx, 1), self.x2.at[k, hi], self.X3_OUT, self.X3_IN, p.x).wait_recv()
        add_into(self.part.at[zz], self.x2.at[k], p.b * self.quarter, self.quarter)
        self.hop(zz, self.at(p.by, 0), self.y2.at[k, lo], self.Y3_OUT, self.Y3_IN, p.y).wait_recv()
        add_into(self.part.at[zz], self.y2.at[k], p.b * self.quarter, self.quarter)

    def z_rows(self, k):
        p = self.p
        rows = self.total // self.z_parts
        return (p.b * self.quarter, self.quarter) if self.wide else (k * rows, rows)

    def z_slot(self, zz, upward, k):
        slot = zz + 1 if upward else zz
        if self.wide:
            return self.zin.at[slot]
        row, rows = self.z_rows(k)
        return self.zin.at[slot, pl.ds(row, rows)]

    def z_hop(self, zz, upward, k):
        p = self.p
        row, rows = self.z_rows(k)
        here = pl.ds(pl.multiple_of(row, 16), rows)
        out, into = (self.Z_UP, self.Z_UP_IN) if upward else (self.Z_DOWN, self.Z_DOWN_IN)
        return p.copy(
            self.part.at[zz, here],
            self.z_slot(zz, upward, k),
            self.z_sems.at[out, zz, k],
            self.z_sems.at[into, zz, k],
            p.up if upward else p.down,
        )

    def z_take(self, zz, upward, k):
        self.z_hop(zz, upward, k).wait_recv()
        row, rows = self.z_rows(k)
        src = self.z_slot(zz, upward, k)
        if not self.wide:
            slot = zz + 1 if upward else zz
            fetch = pltpu.make_async_copy(src, self.stage, self.z_sems.at[self.FETCH, slot, k])
            fetch.start()
            fetch.wait()
            src = self.stage
        add_into(self.part.at[zz], src, row, rows)

    def z_step(self, d, k=0):
        p = self.p
        for upward, there, exists, inner in (
            (True, p.z + d, p.z + d < p.planes, p.has_down),
            (False, p.z - d, p.z >= d, p.has_up),
        ):
            pl.when(jnp.logical_and(exists, inner))(
                lambda there=there, upward=upward: self.z_take(there, upward, k)
            )
            p.send(lambda there=there, upward=upward: self.z_hop(there, upward, k), exists)

    def z_last(self, k=0):
        p = self.p
        pl.when(p.has_down)(lambda: self.z_take(p.z, True, k))
        pl.when(p.has_up)(lambda: self.z_take(p.z, False, k))

    def z_steps(self):
        for k in range(self.z_parts):
            for d in range(self.p.planes - 1, 0, -1):
                yield functools.partial(self.z_step, d, k)
            yield functools.partial(self.z_last, k)

    def plane_steps(self, zz):
        if self.p.square:
            yield functools.partial(self.plane_2, zz)
            yield functools.partial(self.plane_3, zz)

    def spread_steps(self):
        yield self.spread_1
        yield self.spread_2
        yield self.spread_3

    def last_hop(self, src, rows, out, into, device):
        return self.p.copy(
            src, self.out.at[rows], self.last_sems.at[out], self.last_sems.at[into], device
        )

    def spread_1(self):
        p = self.p
        if not p.square:
            pltpu.make_async_copy(self.part.at[p.z], self.out, self.last_sems.at[self.LOCAL]).start()
            return
        rows = self.at(p.b)
        src = self.part.at[p.z, rows]
        p.send(lambda: self.last_hop(src, rows, self.GX_OUT, self.GX_IN, p.x))
        p.send(lambda: self.last_hop(src, rows, self.GY_OUT, self.GY_IN, p.y))
        pltpu.make_async_copy(src, self.out.at[rows], self.last_sems.at[self.LOCAL]).start()

    def spread_2(self):
        p = self.p
        if not p.square:
            return
        from_x, from_y = self.at(p.bx), self.at(p.by)
        half_x, half_y = self.at(p.bx, 0), self.at(p.by, 1)
        self.last_hop(self.out.at[from_x], from_x, self.GX_OUT, self.GX_IN, p.x).wait_recv()
        p.send(lambda: self.last_hop(self.out.at[half_x], half_x, self.FY_OUT, self.FY_IN, p.y))
        self.last_hop(self.out.at[from_y], from_y, self.GY_OUT, self.GY_IN, p.y).wait_recv()
        p.send(lambda: self.last_hop(self.out.at[half_y], half_y, self.FX_OUT, self.FX_IN, p.x))

    def spread_3(self):
        p = self.p
        if not p.square:
            pltpu.make_async_copy(self.part.at[p.z], self.out, self.last_sems.at[self.LOCAL]).wait()
            return
        rows = self.at(p.b)
        half_0, half_1 = self.at(p.bd, 0), self.at(p.bd, 1)
        self.last_hop(self.out.at[half_0], half_0, self.FY_OUT, self.FY_IN, p.y).wait_recv()
        self.last_hop(self.out.at[half_1], half_1, self.FX_OUT, self.FX_IN, p.x).wait_recv()
        pltpu.make_async_copy(
            self.part.at[p.z, rows], self.out.at[rows], self.last_sems.at[self.LOCAL]
        ).wait()


def dot(a, b):
    return jnp.dot(a, b, preferred_element_type=F32)


def dot_nt(a, b):
    return lax.dot_general(a, b, (((1,), (1,)), ((), ())), preferred_element_type=F32)


def dot_tn(a, b):
    return lax.dot_general(a, b, (((0,), (0,)), ((), ())), preferred_element_type=F32)


def row_loop(rows, chunk, body):
    def step(i, _):
        body(pl.ds(pl.multiple_of(i * chunk, chunk), chunk))
        return 0

    lax.fori_loop(0, rows // chunk, step, 0)


def lanes(block, width=128):
    return pl.ds(pl.multiple_of(block * width, width), width)


def tokens(i, span):
    return pl.ds(pl.multiple_of(i * span, span), span)


def transpose(src, dst):
    rows, cols = src.shape
    whole = cols // 128

    def step(j, _):
        at = lanes(j)
        dst[at, :] = src[:, at].T
        return 0

    lax.fori_loop(0, whole, step, 0)
    if cols % 128:
        dst[whole * 128 :, :] = src[:, whole * 128 :].T


def mean_square(v):
    return jnp.mean(v * v, axis=-1, keepdims=True)


class Pump:
    def __init__(self, steps):
        self.steps = list(steps)

    def __call__(self, count=1):
        for step in self.steps[:count]:
            step()
        del self.steps[:count]

    def until(self, left):
        self(len(self.steps) - left)


def pair_masks(span):
    lane = lax.broadcasted_iota(jnp.int32, (span, 128), 1)
    first = (lane < HEAD_DIM).astype(F32)
    row = lax.broadcasted_iota(jnp.int32, (128, 128), 0)
    col = lax.broadcasted_iota(jnp.int32, (128, 128), 1)
    own = ((row < HEAD_DIM) == (col < HEAD_DIM)).astype(F32)
    return first.astype(BF16), (1.0 - first).astype(BF16), own.astype(BF16), own


def by_head(pair, first, second):
    return jnp.concatenate([pair * first, pair * second], axis=0)


def pack_state(state):
    lane = lax.broadcasted_iota(jnp.int32, (HEAD_DIM, 128), 1)
    return jnp.where(lane < HEAD_DIM, state[:HEAD_DIM], state[HEAD_DIM:])


def unpack_state(packed, own):
    return jnp.concatenate([packed, packed], axis=0) * own


def head_sums(v, own):
    high = v.astype(BF16)
    low = (v - high.astype(F32)).astype(BF16)
    return dot(high, own) + dot(low, own)


class Chain:
    S_OUT, S_IN, Z_OUT, Z_IN, P_OUT, P_IN = range(6)

    def __init__(self, place, forward, mine, other, before, out, sems):
        self.p, self.forward = place, forward
        self.mine, self.other, self.before, self.out, self.sems = mine, other, before, out, sems
        self.half = mine.shape[0] // 2
        if forward:
            self.prev, self.next = place.has_down, place.has_up
            self.device, self.counts = place.up, place.c == 1
        else:
            self.prev, self.next = place.has_up, place.has_down
            self.device, self.counts = place.down, place.c == 0

    @staticmethod
    def scratch(count):
        return [pltpu.VMEM((count, HEAD_DIM, 128), BF16)] * 4 + [pltpu.SemaphoreType.DMA((6,))]

    def part(self, core):
        return pl.ds(core * self.half, self.half)

    def sibling_copy(self):
        return self.p.copy(
            self.mine, self.other, self.sems.at[self.S_OUT], self.sems.at[self.S_IN], self.p.sib
        )

    def next_copy(self):
        here = self.part(self.p.c)
        return self.p.copy(
            self.out.at[here], self.before.at[here], self.sems.at[self.Z_OUT],
            self.sems.at[self.Z_IN], self.device,
        )

    def across_copy(self, core):
        here = self.part(core)
        return self.p.copy(
            self.before.at[here], self.before.at[here], self.sems.at[self.P_OUT],
            self.sems.at[self.P_IN], self.p.sib,
        )

    def start(self):
        self.p.send(self.sibling_copy)

        @pl.when(jnp.logical_not(self.prev))
        def _():
            self.before[...] = jnp.zeros_like(self.before)

    def step(self):
        p = self.p
        self.sibling_copy().wait_recv()
        pl.when(self.prev)(lambda: self.next_copy().wait_recv())
        p.send(lambda: self.across_copy(p.c), self.prev)

        @pl.when(self.next)
        def _():
            def body(i, _):
                k = p.c * self.half + i
                total = self.before[k].astype(F32) + self.mine[k].astype(F32)
                self.out[k] = (total + self.other[k].astype(F32)).astype(BF16)
                return 0

            lax.fori_loop(0, self.half, body, 0)

        p.send(self.next_copy, self.next)

    def finish(self, result):
        p = self.p
        pl.when(self.prev)(lambda: self.across_copy(1 - p.c).wait_recv())
        weight = self.counts.astype(F32)

        def body(k, _):
            total = self.before[k].astype(F32) + self.other[k].astype(F32) * weight
            result[k] = total.astype(BF16)
            return 0

        lax.fori_loop(0, result.shape[0], body, 0)


class Locals:
    def __init__(self, sems):
        self.sems, self.used, self.open = sems, 0, []

    def copy(self, src, dst):
        made = pltpu.make_async_copy(src, dst, self.sems.at[self.used])
        self.used += 1
        made.start()
        return made

    def save(self, src, dst):
        self.open.append(self.copy(src, dst))

    def finish(self):
        for made in self.open:
            made.wait()


def load_columns(local, full, rows, dst, stage):
    seq, _, cols = full.shape
    if cols % 128 == 0:
        return [local.copy(full.at[s, rows], dst.at[:, pl.ds(s * cols, cols)]) for s in range(seq)]
    for s in range(seq):
        local.copy(full.at[s, rows], stage.at[pl.ds(0, rows.size)]).wait()
        dst[:, s * cols : (s + 1) * cols] = stage[: rows.size]
    return []


def stream(count, source, slots, sems, body, after=None):
    def fetch(k):
        return pltpu.make_async_copy(source(k), slots.at[lax.rem(k, 2)], sems.at[lax.rem(k, 2)])

    fetch(0).start()

    def step(k, _):
        @pl.when(k + 1 < count)
        def _():
            fetch(k + 1).start()

        fetch(k).wait()
        body(k, lax.rem(k, 2))
        return 0

    if after is None:
        lax.fori_loop(0, count, step, 0)
    else:
        for k in range(count):
            step(jnp.int32(k), 0)
            after(k)


def forward_kernel(batch, seq, spans, *refs):
    (x_hbm, *shards), refs = refs[:5], refs[5:]
    fulls, refs = refs[:4], refs[4:]
    out_hbm, saved, refs = refs[0], refs[1:13], refs[13:]
    (q_out, k_out, v_out, raw_out, att_out, e_out, gated_out, mid_out, nb_out, pair_out, hid_out, na_out) = saved
    (x, na, tmp, q, k, v, raw, att, gated, mid, nb, w_in, w_out, gain, w_pair, tmp_g, tmp_u, pair, hid,
     w_down, res, stage, na_t, gated_t, nb_t, hid_t, mine, other, before, chain_out, early, chain_sems, slot_sems, pair_sems,
     local_sems, gather_sems, gather_local) = refs
    place = Place(batch, seq)
    local = Locals(local_sems)
    load_x = local.copy(x_hbm, x)
    place.barrier()
    gather = Gather(place, shards, fulls, (True, False, True, True), gather_sems, gather_local)
    rows, span = x.shape[0], spans
    per_group = seq // 4
    blocks = rows // span
    pairs = D // 128
    cols_in = w_in.shape[-1]
    half = seq // 2
    first, second, own, own_f = pair_masks(span)
    pump, marks = plan(gather)

    pump(2)
    load_x.wait()

    def norm_rows(r):
        xr = x[r, :].astype(F32)
        na[r, :] = (xr * lax.rsqrt(mean_square(xr) + 1e-6)).astype(BF16)

    row_loop(rows, 32, norm_rows)
    transpose(na, na_t)
    local.save(na_t, na_out)
    pump.until(marks[0])

    dests = (q, k, v, raw)
    for group in range(4):
        dest = dests[group]

        def project(n, slot, group=group, dest=dest):
            tmp[...] = dot(na[...], w_in[slot])
            at = pl.ds(pl.multiple_of(n * cols_in, 128), cols_in)

            def finish_rows(r):
                value = tmp[r, :]
                if group < 2:
                    value = jnp.maximum(value, 0.0) + jnp.log1p(jnp.exp(-jnp.abs(value)))
                dest[r, at] = value.astype(dest.dtype)

            row_loop(rows, 32, finish_rows)

        stream(
            per_group,
            lambda n, group=group: fulls[0].at[group * per_group + n],
            w_in,
            slot_sems,
            project,
        )
        pump(2)

    def state(n, _):
        i, j = lax.div(n, pairs), lax.rem(n, pairs)
        at, block = tokens(i, span), lanes(j)
        mine[n] = pack_state(dot_tn(k[at, block], v[at, block])).astype(BF16)
        return 0

    lax.fori_loop(0, blocks * pairs, state, 0)
    chain = Chain(place, True, mine, other, before, chain_out, chain_sems)
    chain.start()
    for src, dst in ((q, q_out), (k, k_out), (v, v_out)):
        local.save(src, dst)
    pump(2)

    row = lax.rem(lax.broadcasted_iota(jnp.int32, (2 * span, span), 0), span)
    col = lax.broadcasted_iota(jnp.int32, (2 * span, span), 1)
    lane = lax.broadcasted_iota(jnp.int32, (span, 128), 1)

    def inner(n, _):
        i, j = lax.div(n, pairs), lax.rem(n, pairs)
        at, block = tokens(i, span), lanes(j)
        scores = dot_nt(by_head(q[at, block], first, second), k[at, block])
        scores = jnp.where(row >= col, scores, 0.0).astype(BF16)
        both = dot(scores, v[at, block])
        att[at, block] = jnp.where(lane < HEAD_DIM, both[:span], both[span:])
        return 0

    for i in range(blocks):
        lax.fori_loop(i * pairs, (i + 1) * pairs, inner, 0)
        if i == 0:
            chain.step()
        pump(1)

    pump.until(marks[1])
    waits = load_columns(local, fulls[1], pl.ds(0, D), w_out, stage)
    waits += load_columns(local, fulls[1], pl.ds(D, PAD_ROWS), gain, stage)
    chain.finish(early)
    local.save(early, e_out)
    for made in waits:
        made.wait()

    def outer(n, _):
        i, j = lax.div(n, pairs), lax.rem(n, pairs)
        at, block = tokens(i, span), lanes(j)
        a = att[at, block] + dot(q[at, block], unpack_state(early[n], own))
        att[at, block] = a
        unit = a * lax.rsqrt(head_sums(a * a, own) * (1.0 / HEAD_DIM) + 1e-5)
        normed = unit * gain[0:1, block].astype(F32)
        gated[at, block] = (jax.nn.sigmoid(raw[at, block]) * normed).astype(BF16)
        return 0

    lax.fori_loop(0, blocks * pairs, outer, 0)
    pump(1)

    def branch(n, _):
        at = pl.ds(pl.multiple_of(n * 512, 512), 512)
        mid[:, at] = x[:, at].astype(F32) + dot(gated[...], w_out[:, at])
        return 0

    lax.fori_loop(0, D // 512, branch, 0)

    def norm_mid(r):
        m = mid[r, :]
        nb[r, :] = (m * lax.rsqrt(mean_square(m) + 1e-6)).astype(BF16)

    row_loop(rows, 32, norm_mid)
    transpose(gated, gated_t)
    transpose(nb, nb_t)
    for src, dst in ((raw, raw_out), (att, att_out), (gated_t, gated_out), (mid, mid_out), (nb_t, nb_out)):
        local.save(src, dst)
    pump.until(marks[2])

    def fetch_pair(j):
        slot = j % 2
        return [
            pltpu.make_async_copy(
                fulls[2].at[j + side * half], w_pair.at[slot, side], pair_sems.at[slot, side]
            )
            for side in range(2)
        ]

    for made in fetch_pair(0):
        made.start()
    for j in range(half):
        if j + 1 < half:
            for made in fetch_pair(j + 1):
                made.start()
        for made in fetch_pair(j):
            made.wait()
        slot = j % 2
        tmp_g[...] = dot(nb[...], w_pair[slot, 0])
        tmp_u[...] = dot(nb[...], w_pair[slot, 1])

        def finish_pair(r, j=j):
            gate, up = tmp_g[r, :], tmp_u[r, :]
            pair[j, r, :] = gate.astype(BF16)
            pair[j + half, r, :] = up.astype(BF16)
            hid[j, r, :] = (gate * up).astype(BF16)

        row_loop(rows, 32, finish_pair)
        local.save(pair.at[j], pair_out.at[j])
        local.save(pair.at[j + half], pair_out.at[j + half])
        transpose(hid.at[j], hid_t.at[j])
        local.save(hid_t.at[j], hid_out.at[j])
        pump(max(1, (len(pump.steps) - marks[3]) // (half - j)))

    pump.until(marks[3])
    for made in load_columns(local, fulls[3], pl.ds(0, w_down.shape[0]), w_down, stage):
        made.wait()
    width = hid.shape[-1]

    def down(n, _):
        at = pl.ds(pl.multiple_of(n * 512, 512), 512)
        total = mid[:, at]
        for j in range(half):
            total = total + dot(hid[j], w_down[j * width : (j + 1) * width, at])
        res[:, at] = total.astype(BF16)
        return 0

    lax.fori_loop(0, D // 512, down, 0)
    local.save(res, out_hbm)
    pump.until(0)
    local.finish()
    place.finish()


def plan(gather):
    steps = plan_gather(gather, 4)
    marks = []
    kept = []
    for step in steps:
        kept.append(step)
        if getattr(step, "whole", False):
            marks.append(len(kept))
    return Pump(kept), [len(kept) - m for m in marks]


def forward(batch, seq, x, span, shards):
    rows = x.shape[0]
    cols_in, cols_pair = shards[0].shape[1], shards[2].shape[1]
    half = seq // 2
    states = (rows // span) * (D // 128)
    big = jax.ShapeDtypeStruct((rows, D), BF16)
    big_f = jax.ShapeDtypeStruct((rows, D), F32)
    narrow = shards[3].shape[1] % 128 != 0
    any_space = pl.BlockSpec(memory_space=pl.ANY)
    out_shape = [jax.ShapeDtypeStruct((seq, *a.shape), a.dtype) for a in shards]
    out_shape += [big, big, big, big, big, big_f]
    turned = jax.ShapeDtypeStruct((D, rows), BF16)
    out_shape += [jax.ShapeDtypeStruct((states, HEAD_DIM, 128), BF16), turned, big_f, turned]
    out_shape += [
        jax.ShapeDtypeStruct((seq, rows, cols_pair), BF16),
        jax.ShapeDtypeStruct((half, cols_pair, rows), BF16),
        turned,
    ]
    wide, wide_f = pltpu.VMEM((rows, D), BF16), pltpu.VMEM((rows, D), F32)
    pair_f = pltpu.VMEM((rows, cols_pair), F32)
    scratch = [
        wide, wide, pltpu.VMEM((rows, cols_in), F32), wide, wide, wide, wide, wide_f, wide, wide_f, wide,
        pltpu.VMEM((2, D, cols_in), BF16),
        pltpu.VMEM((D, D), BF16),
        pltpu.VMEM((PAD_ROWS, D), BF16),
        pltpu.VMEM((2, 2, D, cols_pair), BF16),
        pair_f, pair_f,
        pltpu.VMEM((seq, rows, cols_pair), BF16),
        pltpu.VMEM((half, rows, cols_pair), BF16),
        pltpu.VMEM((FF, D), BF16),
        wide,
        pltpu.VMEM((FF, shards[3].shape[1]) if narrow else (16, 128), BF16),
        *[pltpu.VMEM((D, rows), BF16)] * 3,
        pltpu.VMEM((half, cols_pair, rows), BF16),
        *[pltpu.VMEM((states, HEAD_DIM, 128), BF16)] * 5,
        pltpu.SemaphoreType.DMA((6,)),
        pltpu.SemaphoreType.DMA((2,)),
        pltpu.SemaphoreType.DMA((2, 2)),
        pltpu.SemaphoreType.DMA((128,)),
        pltpu.SemaphoreType.DMA((Gather.KINDS, 4, half)),
        pltpu.SemaphoreType.DMA((4,)),
    ]
    return pl.pallas_call(
        functools.partial(forward_kernel, batch, seq, span),
        out_shape=out_shape,
        in_specs=[any_space] * 5,
        out_specs=[any_space] * len(out_shape),
        scratch_shapes=scratch,
        compiler_params=pltpu.CompilerParams(
            collective_id=0, has_side_effects=True, vmem_limit_bytes=62 * 1024 * 1024
        ),
        name="forward",
    )(x, *shards)


WIDE = (False, True, False, True)
Z_PARTS = (4, 4, 2, 4)


def slope(plus):
    series = plus * (1.0 - plus * (0.5 - plus * (1.0 / 6.0)))
    return jnp.where(plus < 0.02, series, 1.0 - jnp.exp(-plus))


def backward_kernel(batch, seq, span, *refs):
    g_hbm, x_hbm, *fulls = refs[:6]
    (q_in, k_in, v_in, raw_in, att_in, e_in, gated_in, mid_in, nb_in, pair_in, hid_in, na_in) = refs[6:18]
    grad_hbm, sums, gm_hbm, far = refs[18], refs[19:23], refs[23], refs[24:28]
    refs = list(refs[28:])
    place = Place(batch, seq)
    reds = []
    for w in range(4):
        reds.append(Reduce(place, WIDE[w], Z_PARTS[w], sums[w], far[w], refs[:11]))
        refs = refs[11:]
    (tall, turned, pair, fields, f0, f1, g, split, low, down, slots, wide_out, slim_out, gain, gain_sums, gain_split,
     early, mine, other, before, chain_out, stage, chain_sems, slot_sems, local_sems) = refs
    red_down, red_pair, red_out, red_in = reds
    local = Locals(local_sems)
    rows = g.shape[0]
    half = seq // 2
    planes = half
    width = hid_in.shape[1]
    cols_in, cols_out, cols_pair = fulls[0].shape[2], fulls[1].shape[2], fulls[2].shape[2]
    per_group, per_block = seq // 4, cols_in // 128
    blocks, pairs = rows // span, D // 128
    first, second, own, own_f = pair_masks(span)
    core, sibling = place.c, 1 - place.c
    pending = Pump([])

    load_g = local.copy(g_hbm, g)
    load_hid = [local.copy(hid_in.at[j], tall.at[pl.ds(j * width, width)]) for j in range(half)]
    load_nb = local.copy(nb_in, turned)
    load_pair = [local.copy(pair_in.at[s], pair.at[s]) for s in range(seq)]
    load_mid = local.copy(mid_in, f1)
    load_e = local.copy(e_in, early)
    place.barrier()

    def split_columns(src):
        for s in range(seq):
            to = (s % 2) * (D // 2) + (s // 2) * cols_out
            split[:, to : to + cols_out] = src[:, s * cols_out : (s + 1) * cols_out]

    def by_core(which):
        return pl.ds(pl.multiple_of(which * (D // 2), D // 2), D // 2)

    slim_sent = []

    def slim_send(red, row, count, k, fill):
        slot = len(slim_sent) % 2
        if len(slim_sent) >= 2:
            for made in slim_sent[-2]:
                made().wait_send()
        fill(slot)
        sent = []
        for zz in range(planes):
            src = slim_out.at[slot, zz, pl.ds(0, count)]
            sent.append(functools.partial(red.core_copy, zz, src, row, count, k))
            sent[-1]().start()
        slim_sent.append(sent)

    def slim_theirs(red, lhs, at, row, count, k):
        def fill(slot):
            value = dot(lhs[at : at + count, :], split[:, by_core(sibling)])
            for zz in range(planes):
                slim_out[slot, zz, 0:count, :] = value[:, zz * cols_out : (zz + 1) * cols_out].astype(BF16)

        slim_send(red, row, count, k, fill)

    def slim_mine(red, lhs, at, row, count, k):
        value = dot(lhs[at : at + count, :], split[:, by_core(core)])
        for zz in range(planes):
            red.core_copy(zz, None, row, count, k).wait_recv()
            here = red.part[zz, row : row + count, :].astype(F32)
            here = here + value[:, zz * cols_out : (zz + 1) * cols_out]
            red.part[zz, row : row + count, :] = here.astype(BF16)

    wide_sent = []

    def wide_theirs(red, cols, zz):
        slot = len(wide_sent) % 2
        if len(wide_sent) >= 2:
            wide_sent[-2]().wait_send()
        s = 2 * zz + sibling

        def body(r):
            wide_out[slot, r, 0:cols] = dot(turned[r, :], pair[s, :, 0:cols]).astype(BF16)

        row_loop(D, 256, body)
        src = wide_out.at[slot] if cols == wide_out.shape[2] else wide_out.at[slot, :, pl.ds(0, cols)]
        wide_sent.append(functools.partial(red.core_copy, zz, src, 0, D, 0))
        wide_sent[-1]().start()

    def wide_mine(red, cols, zz):
        s = 2 * zz + core
        red.core_copy(zz, None, 0, D, 0).wait_recv()

        def body(r):
            here = red.part[zz, r, :].astype(F32) + dot(turned[r, :], pair[s, :, 0:cols])
            red.part[zz, r, :] = here.astype(BF16)

        row_loop(D, 256, body)
        if red.wide:
            red.plane_1(zz)

    load_g.wait()
    split_columns(g)
    for made in load_hid:
        made.wait()
    for j in range(half):
        slim_theirs(red_down, tall, j * width, j * width, width, j)
    for j in range(half):
        slim_mine(red_down, tall, j * width, j * width, width, j)
    pending.steps += red_down.z_steps()

    def load_down(j):
        at = pl.ds((j % 2) * width, width)
        return load_columns(local, fulls[3], pl.ds(j * width, width), down.at[at], stage)

    for made in load_pair:
        made.wait()
    waits = load_down(0)
    for j in range(half):
        after = load_down(j + 1) if j + 1 < half else []
        for made in waits:
            made.wait()
        waits = after
        at = (j % 2) * width
        f0[:, 0:width] = dot_nt(g[...], down[at : at + width, :])

        def finish_pair(r, j=j):
            grad = f0[r, 0:width]
            gate, up = pair[j, r, :].astype(F32), pair[j + half, r, :].astype(F32)
            pair[j, r, :] = (grad * up).astype(BF16)
            pair[j + half, r, :] = (grad * gate).astype(BF16)

        row_loop(rows, 32, finish_pair)

    load_nb.wait()
    wide_theirs(red_pair, cols_pair, 0)
    for zz in range(planes):
        if zz + 1 < planes:
            wide_theirs(red_pair, cols_pair, zz + 1)
        wide_mine(red_pair, cols_pair, zz)
        pending.steps += red_pair.plane_steps(zz)
        pending(1)
    load_gated = local.copy(gated_in, turned)
    w_out = down.at[pl.ds(0, D)]
    load_out = load_columns(local, fulls[1], pl.ds(0, D), w_out, stage)
    load_out += load_columns(local, fulls[1], pl.ds(D, PAD_ROWS), gain, stage)
    views = []
    for k, src in enumerate((q_in, k_in, v_in, raw_in)):
        for side in range(2):
            to = tall.at[pl.ds((2 * k + side) * rows, rows)]
            views.append(local.copy(src.at[:, pl.ds(side * (D // 2), D // 2)], to))

    f0[...] = jnp.zeros_like(f0)

    def back_pair(s, slot):
        f0[...] += dot_nt(pair[s], slots[slot])

    stream(seq, lambda s: fulls[2].at[s], slots, slot_sems, back_pair, lambda s: pending(1))
    load_mid.wait()

    def back_mid(r):
        m, grad = f1[r, :], f0[r, :]
        scale = lax.rsqrt(mean_square(m) + 1e-6)
        inner = jnp.mean(grad * m, axis=-1, keepdims=True)
        total = g[r, :].astype(F32) + scale * grad - m * (scale * scale * scale) * inner
        f1[r, :] = total
        low[r, :] = total.astype(BF16)

    row_loop(rows, 32, back_mid)
    save_gm = local.copy(f1, gm_hbm)
    split_columns(low)

    load_gated.wait()
    for k in range(2):
        slim_theirs(red_out, turned, k * (D // 2), k * (D // 2), D // 2, k)
    for k in range(2):
        slim_mine(red_out, turned, k * (D // 2), k * (D // 2), D // 2, k)
    load_na = local.copy(na_in, turned)
    pending(2)
    for made in load_out:
        made.wait()

    def back_branch(n, _):
        at = pl.ds(pl.multiple_of(n * 512, 512), 512)
        f0[:, at] = dot_nt(low[...], w_out[at, :])
        return 0

    lax.fori_loop(0, D // 512, back_branch, 0)
    load_x = local.copy(x_hbm, low)
    save_gm.wait()
    load_att = local.copy(att_in, f1)
    gain_sums[...] = jnp.zeros_like(gain_sums)
    for made in views:
        made.wait()
    load_att.wait()
    load_e.wait()

    def view(k, i, j):
        row = (2 * k + lax.div(j, pairs // 2)) * rows + i * span
        return tokens_at(row, span), lanes(lax.rem(j, pairs // 2))

    def tokens_at(row, count):
        return pl.ds(pl.multiple_of(row, count), count)

    def put(group, i, j, value):
        s = group * per_group + lax.div(j, per_block)
        pair[s, tokens(i, span), lanes(lax.rem(j, per_block))] = value.astype(BF16)

    def back_gate(n, _):
        i, j = lax.div(n, pairs), lax.rem(n, pairs)
        at, block = tokens(i, span), lanes(j)
        a, grad = f1[at, block], f0[at, block]
        scale = lax.rsqrt(head_sums(a * a, own) * (1.0 / HEAD_DIM) + 1e-5)
        unit = a * scale
        gains = gain[0:1, block].astype(F32)
        sig = jax.nn.sigmoid(tall[view(3, i, j)].astype(F32))
        grad_normed = grad * sig
        put(3, i, j, grad * (unit * gains) * sig * (1.0 - sig))
        gain_sums[0:1, block] += jnp.sum(grad_normed * unit, axis=0, keepdims=True)
        grad_unit = grad_normed * gains
        inner = head_sums(grad_unit * a, own) * (1.0 / HEAD_DIM)
        grad_a = (scale * grad_unit - a * (scale * scale * scale) * inner).astype(BF16)
        g[at, block] = grad_a
        mine[n] = pack_state(dot_tn(tall[view(0, i, j)], grad_a)).astype(BF16)
        return 0

    lax.fori_loop(0, blocks * pairs, back_gate, 0)
    chain = Chain(place, False, mine, other, before, chain_out, chain_sems)
    chain.start()

    for s in range(seq):
        to = (s // 2) * cols_out
        gain_split[s % 2, :, to : to + cols_out] = gain_sums[:, s * cols_out : (s + 1) * cols_out]
    top = lax.broadcasted_iota(jnp.int32, (GAIN_ROWS, cols_out), 0) == 0

    def gain_rows(which, zz):
        row = gain_split[which, 0:1, zz * cols_out : (zz + 1) * cols_out]
        return jnp.where(top, row, 0.0)

    def fill_gain(slot):
        for zz in range(planes):
            slim_out[slot, zz, 0:GAIN_ROWS, :] = gain_rows(sibling, zz).astype(BF16)

    slim_send(red_out, D, GAIN_ROWS, 2, fill_gain)
    load_na.wait()
    last = planes - 1
    ready = [zz for zz in range(planes) if zz * 2 >= 3 * per_group]
    for zz in ready:
        wide_theirs(red_in, cols_in, zz)
    for zz in range(planes):
        red_out.core_copy(zz, None, D, GAIN_ROWS, 2).wait_recv()
        here = red_out.part[zz, D : D + GAIN_ROWS, :].astype(F32) + gain_rows(core, zz)
        red_out.part[zz, D : D + GAIN_ROWS, :] = here.astype(BF16)
    for zz in ready:
        wide_mine(red_in, cols_in, zz)
    chain.step()
    pending.steps += red_out.z_steps()

    t_of = lax.rem(lax.broadcasted_iota(jnp.int32, (span, 2 * span), 1), span)
    s_of = lax.broadcasted_iota(jnp.int32, (span, 2 * span), 0)
    t_down = lax.rem(lax.broadcasted_iota(jnp.int32, (2 * span, span), 0), span)
    s_down = lax.broadcasted_iota(jnp.int32, (2 * span, span), 1)
    lane = lax.broadcasted_iota(jnp.int32, (span, 128), 1)

    def back_attention(n, _):
        i, j = lax.div(n, pairs), lax.rem(n, pairs)
        at, block = tokens(i, span), lanes(j)
        qs, ks, vs = (tall[view(k, i, j)] for k in range(3))
        grads = g[at, block]
        q2, g2 = by_head(qs, first, second), by_head(grads, first, second)
        scores = jnp.where(t_of >= s_of, dot_nt(ks, q2), 0.0).astype(BF16)
        grad_t = jnp.where(t_of >= s_of, dot_nt(vs, g2), 0.0).astype(BF16)
        grad_s = jnp.where(t_down >= s_down, dot_nt(g2, vs), 0.0).astype(BF16)
        both = dot(grad_s, ks)
        grad_q = jnp.where(lane < HEAD_DIM, both[:span], both[span:])
        grad_q = grad_q + dot_nt(grads, unpack_state(early[n], own))
        f0[at, block] = dot(grad_t, q2)
        f1[at, block] = dot(scores, g2)
        put(0, i, j, grad_q * slope(qs.astype(F32)))
        return 0

    for i in range(blocks):
        lax.fori_loop(i * pairs, (i + 1) * pairs, back_attention, 0)
        pending(2)
    ready_q = [zz for zz in range(planes) if (zz + 1) * 2 <= per_group]
    for zz in ready_q:
        wide_theirs(red_in, cols_in, zz)
    for zz in ready_q:
        wide_mine(red_in, cols_in, zz)
    chain.finish(other)

    def back_states(n, _):
        i, j = lax.div(n, pairs), lax.rem(n, pairs)
        at, block = tokens(i, span), lanes(j)
        ks, vs = tall[view(1, i, j)], tall[view(2, i, j)]
        later = unpack_state(other[n], own)
        grad_k = f0[at, block] + dot_nt(vs, later)
        put(1, i, j, grad_k * slope(ks.astype(F32)))
        put(2, i, j, f1[at, block] + dot(ks, later))
        return 0

    lax.fori_loop(0, blocks * pairs, back_states, 0)
    load_gm = local.copy(gm_hbm, f1)
    rest = [zz for zz in range(planes) if zz not in ready and zz not in ready_q]
    for n, zz in enumerate(rest):
        wide_theirs(red_in, cols_in, zz)
        if n:
            wide_mine(red_in, cols_in, rest[n - 1])
    if rest:
        wide_mine(red_in, cols_in, rest[-1])
    for red in (red_down, red_out):
        if place.square:
            pending.steps.append(functools.partial(red.plane_1, place.z))
    for red in (red_down, red_out):
        pending.steps += red.plane_steps(place.z)
    for red in (red_down, red_out):
        pending.steps.append(red.spread_1)
    pending.steps += red_pair.z_steps()
    pending.steps.append(red_pair.spread_1)
    for zz in ready + ready_q + rest:
        pending.steps += red_in.plane_steps(zz)
    pending.steps += red_in.z_steps()
    pending.steps.append(red_in.spread_1)
    for name in ("spread_2", "spread_3"):
        for red in (red_down, red_out, red_pair, red_in):
            pending.steps.append(getattr(red, name))

    f0[...] = jnp.zeros_like(f0)
    w_in = slots if cols_in == slots.shape[2] else slots.at[:, :, pl.ds(0, cols_in)]

    def back_in(s, slot):
        f0[...] += dot_nt(pair[s, :, 0:cols_in], w_in[slot])

    stream(seq, lambda s: fulls[0].at[s], w_in, slot_sems, back_in, lambda s: pending(3))
    load_gm.wait()
    load_x.wait()

    def back_x(r):
        x, grad = low[r, :].astype(F32), f0[r, :]
        scale = lax.rsqrt(mean_square(x) + 1e-6)
        inner = jnp.mean(grad * x, axis=-1, keepdims=True)
        f1[r, :] += scale * grad - x * (scale * scale * scale) * inner

    row_loop(rows, 32, back_x)
    local.save(f1, grad_hbm)
    pending.until(0)
    local.finish()
    for sent in slim_sent[-2:]:
        for made in sent:
            made().wait_send()
    for made in wide_sent[-2:]:
        made().wait_send()
    place.finish()


def backward(batch, seq, span, grad, x, fulls, saved):
    rows = x.shape[0]
    half = seq // 2
    cols_in, cols_out, cols_pair = fulls[0].shape[2], fulls[1].shape[2], fulls[2].shape[2]
    width = saved[10].shape[1]
    square = batch == 4
    shapes = ((FF, cols_out), (D, cols_pair), (D + GAIN_ROWS, cols_out), (D, cols_in))
    states = (rows // span) * (D // 128)
    any_space = pl.BlockSpec(memory_space=pl.ANY)
    big_f = jax.ShapeDtypeStruct((rows, D), F32)
    out_shape = [big_f] + [jax.ShapeDtypeStruct(shape, BF16) for shape in shapes] + [big_f]
    out_shape += [Reduce.far(square, WIDE[w], half, *shapes[w]) for w in range(4)]
    scratch = []
    core_parts = (half, 1, 3, 1)
    for w in range(4):
        scratch += Reduce.scratch(square, WIDE[w], half, *shapes[w], core_parts[w], Z_PARTS[w])
    narrow = cols_out % 128 != 0
    state = pltpu.VMEM((states, HEAD_DIM, 128), BF16)
    scratch += [
        pltpu.VMEM((max(FF, 8 * rows), D // 2), BF16),
        pltpu.VMEM((D, rows), BF16),
        pltpu.VMEM((seq, rows, cols_pair), BF16),
        pltpu.VMEM((16, 128), BF16),
        pltpu.VMEM((rows, D), F32),
        pltpu.VMEM((rows, D), F32),
        pltpu.VMEM((rows, D), BF16),
        pltpu.VMEM((rows, D), BF16),
        pltpu.VMEM((rows, D), BF16),
        pltpu.VMEM((max(2 * width, D), D), BF16),
        pltpu.VMEM((2, D, cols_pair), BF16),
        pltpu.VMEM((2, D, cols_pair), BF16),
        pltpu.VMEM((2, half, max(width, D // 2), cols_out), BF16),
        pltpu.VMEM((PAD_ROWS, D), BF16),
        pltpu.VMEM((8, D), F32),
        pltpu.VMEM((2, 8, D // 2), F32),
        state, state, state, state, state,
        pltpu.VMEM((D, cols_out) if narrow else (16, 128), BF16),
        pltpu.SemaphoreType.DMA((6,)),
        pltpu.SemaphoreType.DMA((2,)),
        pltpu.SemaphoreType.DMA((192,)),
    ]
    return pl.pallas_call(
        functools.partial(backward_kernel, batch, seq, span),
        out_shape=out_shape,
        in_specs=[any_space] * 18,
        out_specs=[any_space] * len(out_shape),
        scratch_shapes=scratch,
        compiler_params=pltpu.CompilerParams(
            collective_id=1, has_side_effects=True, vmem_limit_bytes=63 * 1024 * 1024
        ),
        name="backward",
    )(grad, x, *fulls, *saved)


def local(block_in, attn_in, attn_out, out_gain, glu_in, glu_out, block_grad):
    seq_count, span = block_in.shape[:2]
    rows = seq_count * span
    batch, seq = lax.axis_size("batch"), lax.axis_size("seq")
    x = block_in.reshape(rows, D)
    with_gain = jnp.concatenate([attn_out, jnp.broadcast_to(out_gain, (PAD_ROWS, out_gain.shape[0]))])
    parts = forward(batch, seq, x, span, (attn_in, with_gain, glu_in, glu_out))
    fulls, block_out, saved = parts[:4], parts[4], parts[5:]
    grads = backward(batch, seq, span, block_grad.reshape(rows, D), x, fulls, saved)
    input_grad, sums = grads[0], list(grads[1:5])
    if batch != 4:
        sums = [lax.psum(a, "batch") for a in sums]
    down, pair, out, into = (a.astype(F32) for a in sums)
    return (
        block_out.reshape(block_in.shape),
        input_grad.reshape(block_in.shape),
        into,
        out[:D],
        out[D],
        pair,
        down,
    )


def solution(mesh):
    rows, columns = P("batch", "seq", None), P(None, "seq")
    return jax.shard_map(
        local,
        mesh=mesh,
        in_specs=(rows, columns, columns, P("seq"), columns, columns, rows),
        out_specs=(rows, rows, columns, columns, P("seq"), columns, columns),
        check_vma=False,
    )
```

time: 960 us -> 525 us (0.55)
  waiting for transfers between devices: 610 us -> 0 us
  Pallas kernels: 0 us -> 503 us
  matrix products: 133 us -> 0 us
  local copies, waits for them, and re-layouts: 89.8 us -> 11.1 us
  other arithmetic: 68.9 us -> 5.48 us
  blocking collectives: 33 us -> 0 us
  between operations: 15.5 us -> 0.94 us
    pallas_call x0 -> x2, Pallas kernels: none -> 503 us  [the longest x1 334 us: backward(): pl.pallas_call(functools.partial(backward_kernel, batch, seq, span), out_...]
    all_gather x6 -> x0, waiting for transfers between devices: 305 us -> none  [the longest x1 95.8 us: local(): lax.all_gather(glu_in, 'seq', axis=1, tiled=True)]
    reduce_scatter x2 -> x0, waiting for transfers between devices: 208 us -> none  [the longest x1 118 us: local(): lax.psum_scatter(glu_in_grad.astype(jnp.bfloat16), 'seq', scatter_dimensi...]
    dot_general x24 -> x0, matrix products: 133 us -> none  [the longest x1 13.3 us: local(): jnp.einsum('rd,fd->rf', grad_out, w_glu_out, preferred_element_type=jnp.f...]
    reshape x16 -> x0, local copies, waits for them, and re-layouts: 60.4 us -> none  [the longest x2 9.02 us: local(): grad_key.reshape(row_count, D) * jax.nn.sigmoid(key_raw)]
    psum x1 -> x0, waiting for transfers between devices: 51.6 us -> none  [local(): lax.psum(grad_parts[0].astype(jnp.bfloat16), 'batch').astype(jnp.float32)]
    unnamed x13 -> x0, waiting for transfers between devices: 46.3 us -> none
    select_n x16 -> x0, other arithmetic: 40.4 us -> none  [step(): return jnp.where(reached, new, before)]
  transfers between devices with their start and end apart: 11 -> 0, of which waited for: 9 -> 0; matrix products, arithmetic and copies ran while one was open for 22% -> 0% of each run, Pallas kernels for 0% -> 0%
where the time goes in v1:
time: 525 us; the launch traced here: 521 us
  Pallas kernels  503 us (96%)
  local copies, waits for them, and re-layouts  11.1 us (2%)
  other arithmetic  5.48 us (1%)
    pallas_call x1, Pallas kernels, backward(): pl.pallas_call(functools.partial(backward_kernel, batch, seq, span), out_...  334 us
    pallas_call x1, Pallas kernels, forward(): pl.pallas_call(functools.partial(forward_kernel, batch, seq, span), out_s...  169 us

profile of v1, /device:TPU:0, one launch (start us, length us, event | category | flops | bytes accessed | tf_op | source)
XLA Modules:
  0.0 520.9 jit_solution(12149521707024211180)
XLA Ops:
  0.6 0.7 broadcast_in_dim.3
  1.3 1.7 pad_maximum_fusion.refs_2_
  3.0 2.6 copy.14.refs_3_
  5.5 169.3 %forward.1 = (bf16[8,1024,512]{2,1,0:T(8,128)(2,1)}, bf16[8,1040,128]{2,1,0:T(8,128)(2,1)}, bf16[8,1024,704]{2,1,0:T(8,128)(2,1)}, bf16[8,2816,128]{2,1,0:T(8,12...) custom-call(bf16[512,1024]{1,0:T(8,128)(2,1)} %bitcast.6, ...), custom_call_target="tpu_custom_call" | custom-call | tf_op jit(solution)/shard_map/forward/pallas_call | solution.py:908
  174.8 334.1 %backward.1 = (f32[512,1024]{1,0:T(8,128)}, bf16[2816,128]{1,0:T(8,128)(2,1)}, bf16[1024,704]{1,0:T(8,128)(2,1)}, bf16[1152,128]{1,0:T(8,128)(2,1)}, bf16[1024,5...) custom-call(bf16[512,1024]{1,0:T(8,128)(2,1)} %bitcast.9, ...), custom_call_target="tpu_custom_call" | custom-call | tf_op jit(solution)/shard_map/backward/pallas_call | solution.py:1325
  508.9 0.0 copy-start.4
  509.0 0.0 copy-start.2
  509.0 1.9 slice.8
  510.9 1.0 convert_element_type.13
  511.9 0.5 slice_bitcast_fusion
  512.4 0.0 copy-done.4
  512.4 1.2 convert_element_type.15
  513.6 0.0 copy-done.2
  513.6 0.0 copy-start.1
  513.6 1.6 convert_element_type.12
  515.2 0.2 copy-done.1
  515.4 0.0 copy-start.3
  515.4 2.0 copy.15
  517.4 0.0 copy-done.3
  517.4 0.0 copy-start
  517.4 1.0 copy.18
  518.3 1.0 copy-done
  519.3 1.3 copy.19
Async XLA Ops:
  508.9 3.4 copy-start.4
  509.0 4.6 copy-start.2
  513.6 1.8 copy-start.1
  515.4 2.0 copy-start.3
  517.4 2.0 copy-start
